TPU v7x, 32 devices: a whole 2x2x4 slice. The times are simulated.
32 devices in a mesh: col: 8 (over z, x), row: 4 (over y, core).
Axes of the slice: x: 2, y: 2, z: 4, core: 2. Of those that a mesh axis runs over, the one named last changes fastest.
Arguments:
- right_side: float32 [8, 256, 256], P('col'), may hold values from -6 to 6
- coupling: bfloat16 [2, 4, 256, 81920], P(None, 'row', None, 'col'), may hold values from -0.01953125 to 0.01953125
- child_solution: bfloat16 [81920, 256], P(('col', 'row')), may hold values from -6 to 6
- factor_blocks: bfloat16 [2, 4, 256, 8, 256], P(None, 'row', None, 'col'), may hold values from -1 to 1
- pattern: int32 [8, 8], replicated, may hold values from 0 to 1, as said below
- diag_inverse: bfloat16 [8, 256, 256], P('col'), may hold values from -0.375 to 0.375
Outputs:
- solved: bfloat16 [8, 256, 256], P('col')
Inputs may be any that keep to these rules, and one draw needn't show every extreme that they name: pattern[j, j - 1] = 1 for every j from 1 to 7; entries with k >= j are not read.
All inputs are finite; a program needn't handle non-finite values.
Results may differ from a plain program's by a relative error of at most 0.017.
Values may be sent and summed in bfloat16 or wider, within the bound.
A program may use at most 64 MiB of HBM per device.

v0:
```python
import jax
import jax.numpy as jnp
from jax import lax
from jax.sharding import PartitionSpec as P


def per_device(right_side, coupling, child_solution, factor_blocks, pattern, diag_inverse):
    nrow = lax.axis_size("row")
    ncol = lax.axis_size("col")
    row_index = lax.axis_index("row")
    col_index = lax.axis_index("col")
    brows = coupling.shape[0]
    blk_size = coupling.shape[2]
    kcols = coupling.shape[3]
    rhs_count = child_solution.shape[1]
    nblk = pattern.shape[0]
    group = ncol // nblk
    part_rows = blk_size // group
    my_block = col_index // group
    my_offset = col_index % group * part_rows
    flat = coupling.reshape(brows * blk_size, kcols)
    update = jnp.dot(
        flat,
        lax.all_gather(child_solution, "row", axis=0, tiled=True),
        preferred_element_type=jnp.float32,
    )
    update = update.reshape(brows, blk_size, rhs_count)
    rhs_part = right_side.reshape(part_rows, rhs_count)
    placed = lax.dynamic_update_slice(
        jnp.zeros((blk_size, rhs_count), jnp.float32), rhs_part, (my_offset, jnp.int32(0))
    )
    blocks = factor_blocks.reshape(brows, blk_size, part_rows)
    inv_rows = diag_inverse.reshape(part_rows, blk_size)

    def advance(j, solved):
        j_row = j % nrow
        j_arow = j // nrow
        flags = lax.dynamic_index_in_dim(pattern, j, 0, keepdims=False)
        flag = lax.dynamic_index_in_dim(flags, my_block, 0, keepdims=False)
        keep = (flag > 0) & (my_block < j)
        masked = jnp.where(keep, solved, jnp.zeros_like(solved))
        row_blocks = lax.dynamic_index_in_dim(blocks, j_arow, 0, keepdims=False)
        partial_value = jnp.dot(row_blocks, masked, preferred_element_type=jnp.float32)
        partial_value = partial_value + lax.dynamic_index_in_dim(update, j_arow, 0, keepdims=False)
        partial_value = jnp.where(my_block == j, placed, jnp.zeros_like(placed)) - partial_value
        partial_value = jnp.where(row_index == j_row, partial_value, jnp.zeros_like(partial_value))
        total = lax.psum(partial_value, ("col", "row"))
        fresh = jnp.dot(
            inv_rows, total.astype(jnp.bfloat16), preferred_element_type=jnp.float32
        ).astype(jnp.bfloat16)
        return jnp.where(my_block == j, fresh, solved)

    start_state = jnp.zeros((part_rows, rhs_count), jnp.bfloat16)
    solved = lax.fori_loop(0, nblk, advance, start_state)
    return solved.reshape(1, part_rows, rhs_count)


def solution(mesh):
    in_specs = (
        P("col", None, None),
        P(None, "row", None, "col"),
        P(("col", "row"), None),
        P(None, "row", None, "col", None),
        P(),
        P("col", None, None),
    )
    out_specs = P("col", None, None)
    return jax.shard_map(
        per_device, mesh=mesh, in_specs=in_specs, out_specs=out_specs, check_vma=False
    )
```

profile of v0, /device:TPU:0, one launch (start us, length us, event | category | flops | bytes accessed | tf_op | source)
XLA Modules:
  0.0 424.0 jit_solution(1928758109962869587)
XLA Ops:
  6.5 0.0 all-gather.2.cloned.1.call-start
  6.5 0.7 all-gather.2.cloned.1.call-update
  7.3 1.1 copy.7
  8.4 0.0 copy-start
  8.4 0.0 copy-start.1
  8.4 43.7 %all-gather.2.cloned.1.call-done = bf16[10240,256]{1,0:T(8,128)(2,1)} async-done(((bf16[2560,256]{1,0:T(8,128)(2,1)}), bf16[10240,256]{1,0:T(8,128)(2,1)}) %all-gather.2.cloned.1.call-update) | async-done | bytes 5242896 | tf_op jit(solution)/shard_map/all_gather | solution.py:24
  52.1 8.4 %fusion.12 = f32[2,256,256]{1,2,0:T(8,128)S(1)} fusion(bf16[2,1,256,10240]{3,2,1,0:T(8,128)(2,1)} %param.9, bf16[10240,256]{1,0:T(8,128)(2,1)} %all-gather.2.cloned.1.call-done), kind=kOutput, calls=%fused_computation.15 | convolution fusion | flops 2684354560 | bytes 16252928 | tf_op jit(solution)/shard_map/dot_general | solution.py:22
  60.5 0.0 copy-done
  60.5 0.0 copy-done.1
  60.5 355.9 %while.17 = (s32[]{:T(128)}, bf16[256,256]{0,1:T(8,128)(2,1)S(1)}, s32[]{:T(128)}, s32[]{:T(128)}, f32[256,256]{0,1:T(8,128)S(1)}, /*index=5*/bf16[2,256,256]{2,...) while((s32[]{:T(128)}, bf16[256,256]{0,1:T(8,128)(2,1)S(1)}, ...), condition=%wide.region_2.3_spmd.clone, body=%wide.region_0.2_spmd.clone.sunk | while | flops 67764248 | bytes 1969544 | solution.py:54
  60.5 1.3 dynamic_slice.47
  62.5 0.2 fusion.27
  62.7 42.9 %all-reduce.1 = bf16[256,256]{0,1:T(8,128)(2,1)S(1)} all-reduce(f32[256,256]{0,1:T(8,128)S(1)} %fusion.27), channel_id=1, replica_groups=mesh['col'=8,'row'=4] {'col','row'}, use_global_device_ids=true, to_apply=%region_1.1 | all-reduce | flops 65536 | bytes 393216 | tf_op jit(solution)/shard_map/while/body/eval_jaxpr/psum | solution.py:47
  105.6 0.2 fusion.28
  105.9 1.3 dynamic_slice.47
  107.8 0.2 fusion.27
  108.0 41.9 %all-reduce.1 = bf16[256,256]{0,1:T(8,128)(2,1)S(1)} all-reduce(f32[256,256]{0,1:T(8,128)S(1)} %fusion.27), channel_id=1, replica_groups=mesh['col'=8,'row'=4] {'col','row'}, use_global_device_ids=true, to_apply=%region_1.1 | all-reduce | flops 65536 | bytes 393216 | tf_op jit(solution)/shard_map/while/body/eval_jaxpr/psum | solution.py:47
  150.0 0.2 fusion.28
  150.2 1.3 dynamic_slice.47
  152.2 0.2 fusion.27
  152.4 41.8 %all-reduce.1 = bf16[256,256]{0,1:T(8,128)(2,1)S(1)} all-reduce(f32[256,256]{0,1:T(8,128)S(1)} %fusion.27), channel_id=1, replica_groups=mesh['col'=8,'row'=4] {'col','row'}, use_global_device_ids=true, to_apply=%region_1.1 | all-reduce | flops 65536 | bytes 393216 | tf_op jit(solution)/shard_map/while/body/eval_jaxpr/psum | solution.py:47
  194.2 0.2 fusion.28
  194.5 1.3 dynamic_slice.47
  196.5 0.2 fusion.27
  196.7 41.9 %all-reduce.1 = bf16[256,256]{0,1:T(8,128)(2,1)S(1)} all-reduce(f32[256,256]{0,1:T(8,128)S(1)} %fusion.27), channel_id=1, replica_groups=mesh['col'=8,'row'=4] {'col','row'}, use_global_device_ids=true, to_apply=%region_1.1 | all-reduce | flops 65536 | bytes 393216 | tf_op jit(solution)/shard_map/while/body/eval_jaxpr/psum | solution.py:47
  238.6 0.2 fusion.28
  238.9 1.3 dynamic_slice.47
  240.9 0.2 fusion.27
  241.1 41.8 %all-reduce.1 = bf16[256,256]{0,1:T(8,128)(2,1)S(1)} all-reduce(f32[256,256]{0,1:T(8,128)S(1)} %fusion.27), channel_id=1, replica_groups=mesh['col'=8,'row'=4] {'col','row'}, use_global_device_ids=true, to_apply=%region_1.1 | all-reduce | flops 65536 | bytes 393216 | tf_op jit(solution)/shard_map/while/body/eval_jaxpr/psum | solution.py:47
  282.9 0.2 fusion.28
  283.1 1.3 dynamic_slice.47
  285.1 0.2 fusion.27
  285.3 42.0 %all-reduce.1 = bf16[256,256]{0,1:T(8,128)(2,1)S(1)} all-reduce(f32[256,256]{0,1:T(8,128)S(1)} %fusion.27), channel_id=1, replica_groups=mesh['col'=8,'row'=4] {'col','row'}, use_global_device_ids=true, to_apply=%region_1.1 | all-reduce | flops 65536 | bytes 393216 | tf_op jit(solution)/shard_map/while/body/eval_jaxpr/psum | solution.py:47
  327.3 0.2 fusion.28
  327.6 1.3 dynamic_slice.47
  329.5 0.2 fusion.27
  329.8 41.7 %all-reduce.1 = bf16[256,256]{0,1:T(8,128)(2,1)S(1)} all-reduce(f32[256,256]{0,1:T(8,128)S(1)} %fusion.27), channel_id=1, replica_groups=mesh['col'=8,'row'=4] {'col','row'}, use_global_device_ids=true, to_apply=%region_1.1 | all-reduce | flops 65536 | bytes 393216 | tf_op jit(solution)/shard_map/while/body/eval_jaxpr/psum | solution.py:47
  371.5 0.2 fusion.28
  371.7 1.3 dynamic_slice.47
  373.7 0.2 fusion.27
  373.9 42.2 %all-reduce.1 = bf16[256,256]{0,1:T(8,128)(2,1)S(1)} all-reduce(f32[256,256]{0,1:T(8,128)S(1)} %fusion.27), channel_id=1, replica_groups=mesh['col'=8,'row'=4] {'col','row'}, use_global_device_ids=true, to_apply=%region_1.1 | all-reduce | flops 65536 | bytes 393216 | tf_op jit(solution)/shard_map/while/body/eval_jaxpr/psum | solution.py:47
  416.1 0.2 fusion.28
  416.4 0.8 copy.9
  (1 shorter events, 0.0 us)
Async XLA Ops:
  6.5 45.5 %all-gather.2.cloned.1.call-start = ((), (), s32[]{:S(2)}) async-start(), calls=%async_computation | async-start | bytes 6553600 | tf_op jit(solution)/shard_map/all_gather | solution.py:24
  8.4 52.1 %copy-start = (bf16[2,1,256,1,256]{4,2,3,1,0:T(8,128)(2,1)S(1)}, bf16[2,1,256,1,256]{4,2,3,1,0:T(8,128)(2,1)}, u32[]{:S(2)}) copy-start(bf16[2,1,256,1,256]{4,2,3,1,0:T(8,128)(2,1)} %param.11) | copy-start | bytes 786436
  8.4 52.1 %copy-start.1 = (bf16[1,256,256]{2,1,0:T(8,128)(2,1)S(1)}, bf16[1,256,256]{2,1,0:T(8,128)(2,1)}, u32[]{:S(2)}) copy-start(bf16[1,256,256]{2,1,0:T(8,128)(2,1)} %param.13) | copy-start | bytes 393220
Sparse Core Ops, SparseCore 0:
  8.9 43.1 all-gather.1
where the time goes:
time: 425 us; the launch traced here: 424 us
  blocking collectives  336 us (79%)
  waiting for transfers between devices  44.4 us (10%)
  between operations  13.5 us (3%)
  local copies, waits for them, and re-layouts  12.3 us (3%)
  matrix products  12.1 us (3%)
  loops' own time  5.51 us (1%)
    psum x8, blocking collectives, advance(): total = lax.psum(partial_value, ('col', 'row'))  336 us
    all_gather x1, waiting for transfers between devices, per_device(): lax.all_gather(child_solution, 'row', axis=0, tiled=True)  43.7 us
    dynamic_slice x8, local copies, waits for them, and re-layouts, advance(): flag = lax.dynamic_index_in_dim(flags, my_block, 0, keepdims=False)  10.5 us
  transfers between devices with their start and end apart: 1, of which 1 were waited for; matrix products, arithmetic and copies ran while one was open for 0% of the time, Pallas kernels for 0%

commit v1 on v0

--- a/solution.py
+++ b/solution.py
@@ -44,7 +44,8 @@
         partial_value = partial_value + lax.dynamic_index_in_dim(update, j_arow, 0, keepdims=False)
         partial_value = jnp.where(my_block == j, placed, jnp.zeros_like(placed)) - partial_value
         partial_value = jnp.where(row_index == j_row, partial_value, jnp.zeros_like(partial_value))
-        total = lax.psum(partial_value, ("col", "row"))
+        pieces = lax.all_gather(partial_value, ("col", "row"))
+        total = jnp.sum(pieces, axis=0)
         fresh = jnp.dot(
             inv_rows, total.astype(jnp.bfloat16), preferred_element_type=jnp.float32
         ).astype(jnp.bfloat16)

time: 425 us -> 740 us (1.74)
  waiting for transfers between devices: 44.4 us -> 661 us
  blocking collectives: 336 us -> 0 us
  other arithmetic: 0.01 us -> 31.3 us
    all_gather x0 -> x8, waiting for transfers between devices: none -> 615 us  [advance(): pieces = lax.all_gather(partial_value, ('col', 'row'))]
    psum x8 -> x0, blocking collectives: 336 us -> none  [advance(): total = lax.psum(partial_value, ('col', 'row'))]
    reduce_sum x0 -> x8, other arithmetic: none -> 31.3 us  [advance(): total = jnp.sum(pieces, axis=0)]
  transfers between devices with their start and end apart: 1 -> 9, of which waited for: 1 -> 9; matrix products, arithmetic and copies ran while one was open for 0% -> 0% of each run, Pallas kernels for 0% -> 0%
where the time goes in v1:
time: 740 us; the launch traced here: 739 us
  waiting for transfers between devices  661 us (89%)
  other arithmetic  31.3 us (4%)
  matrix products  16.1 us (2%)
  between operations  13.2 us (2%)
  local copies, waits for them, and re-layouts  11.4 us (2%)
    all_gather x8, waiting for transfers between devices, advance(): pieces = lax.all_gather(partial_value, ('col', 'row'))  615 us
    all_gather x1, waiting for transfers between devices, per_device(): lax.all_gather(child_solution, 'row', axis=0, tiled=True)  44.8 us
    reduce_sum x8, other arithmetic, advance(): total = jnp.sum(pieces, axis=0)  31.3 us
  transfers between devices with their start and end apart: 9, of which 9 were waited for; matrix products, arithmetic and copies ran while one was open for 0% of the time, Pallas kernels for 0%

profile of v1, /device:TPU:0, one launch (start us, length us, event | category | flops | bytes accessed | tf_op | source)
XLA Modules:
  0.0 739.2 jit_solution(12192096462909910116)
XLA Ops:
  6.5 0.7 all-gather.7.cloned.1.call-update
  7.3 0.0 copy-start
  7.3 0.0 copy-start.2
  7.3 0.0 copy-start.3
  7.3 44.8 %all-gather.7.cloned.1.call-done = bf16[10240,256]{1,0:T(8,128)(2,1)} async-done(((bf16[2560,256]{1,0:T(8,128)(2,1)}), bf16[10240,256]{1,0:T(8,128)(2,1)}) %all-gather.7.cloned.1.call-update) | async-done | bytes 5242896 | tf_op jit(solution)/shard_map/all_gather | solution.py:24
  52.1 7.1 fusion.12
  59.2 672.7 %while.17 = (s32[]{:T(128)}, bf16[256,256]{1,0:T(8,128)(2,1)S(1)}, s32[]{:T(128)}, s32[]{:T(128)}, f32[256,256]{1,0:T(8,128)S(1)}, /*index=5*/bf16[2,256,256]{2,...) while((s32[]{:T(128)}, bf16[256,256]{1,0:T(8,128)(2,1)S(1)}, ...), condition=%wide.region_2.3_spmd.clone, body=%wide.region_0.2_spmd.clone.sunk | while | flops 69730328 | bytes 36048312 | solution.py:55
  59.3 0.0 all-gather.9.cloned.1.call-start
  59.3 1.3 dynamic_slice.47
  61.4 0.9 fusion.27
  62.3 0.0 all-gather.9.cloned.1.call-update
  62.3 78.2 %all-gather.9.cloned.1.call-done = f32[8192,256]{1,0:T(8,128)} async-done(((f32[256,256]{1,0:T(8,128)}), f32[8192,256]{1,0:T(8,128)}) %all-gather.9.cloned.1.call-update) | async-done | bytes 8388624 | tf_op jit(solution)/shard_map/while/body/eval_jaxpr/all_gather | solution.py:47
  140.6 3.9 reduce_sum.19
  144.5 0.2 fusion.28
  144.7 0.0 all-gather.9.cloned.1.call-start
  144.8 1.3 dynamic_slice.47
  146.8 0.9 fusion.27
  147.8 0.0 all-gather.9.cloned.1.call-update
  147.8 76.8 %all-gather.9.cloned.1.call-done = f32[8192,256]{1,0:T(8,128)} async-done(((f32[256,256]{1,0:T(8,128)}), f32[8192,256]{1,0:T(8,128)}) %all-gather.9.cloned.1.call-update) | async-done | bytes 8388624 | tf_op jit(solution)/shard_map/while/body/eval_jaxpr/all_gather | solution.py:47
  224.6 3.9 reduce_sum.19
  228.5 0.2 fusion.28
  228.7 0.0 all-gather.9.cloned.1.call-start
  228.8 1.3 dynamic_slice.47
  230.9 0.9 fusion.27
  231.8 0.0 all-gather.9.cloned.1.call-update
  231.8 76.5 %all-gather.9.cloned.1.call-done = f32[8192,256]{1,0:T(8,128)} async-done(((f32[256,256]{1,0:T(8,128)}), f32[8192,256]{1,0:T(8,128)}) %all-gather.9.cloned.1.call-update) | async-done | bytes 8388624 | tf_op jit(solution)/shard_map/while/body/eval_jaxpr/all_gather | solution.py:47
  308.3 3.9 reduce_sum.19
  312.2 0.2 fusion.28
  312.4 0.0 all-gather.9.cloned.1.call-start
  312.5 1.3 dynamic_slice.47
  314.6 0.9 fusion.27
  315.5 0.0 all-gather.9.cloned.1.call-update
  315.5 76.5 %all-gather.9.cloned.1.call-done = f32[8192,256]{1,0:T(8,128)} async-done(((f32[256,256]{1,0:T(8,128)}), f32[8192,256]{1,0:T(8,128)}) %all-gather.9.cloned.1.call-update) | async-done | bytes 8388624 | tf_op jit(solution)/shard_map/while/body/eval_jaxpr/all_gather | solution.py:47
  392.0 3.9 reduce_sum.19
  395.9 0.2 fusion.28
  396.2 0.0 all-gather.9.cloned.1.call-start
  396.3 1.3 dynamic_slice.47
  398.3 0.9 fusion.27
  399.2 0.0 all-gather.9.cloned.1.call-update
  399.2 76.5 %all-gather.9.cloned.1.call-done = f32[8192,256]{1,0:T(8,128)} async-done(((f32[256,256]{1,0:T(8,128)}), f32[8192,256]{1,0:T(8,128)}) %all-gather.9.cloned.1.call-update) | async-done | bytes 8388624 | tf_op jit(solution)/shard_map/while/body/eval_jaxpr/all_gather | solution.py:47
  475.7 3.9 reduce_sum.19
  479.7 0.2 fusion.28
  479.9 0.0 all-gather.9.cloned.1.call-start
  480.0 1.3 dynamic_slice.47
  482.0 0.9 fusion.27
  482.9 0.0 all-gather.9.cloned.1.call-update
  483.0 76.8 %all-gather.9.cloned.1.call-done = f32[8192,256]{1,0:T(8,128)} async-done(((f32[256,256]{1,0:T(8,128)}), f32[8192,256]{1,0:T(8,128)}) %all-gather.9.cloned.1.call-update) | async-done | bytes 8388624 | tf_op jit(solution)/shard_map/while/body/eval_jaxpr/all_gather | solution.py:47
  559.8 3.9 reduce_sum.19
  563.7 0.2 fusion.28
  563.9 0.0 all-gather.9.cloned.1.call-start
  564.0 1.3 dynamic_slice.47
  566.0 0.9 fusion.27
  567.0 0.0 all-gather.9.cloned.1.call-update
  567.0 76.8 %all-gather.9.cloned.1.call-done = f32[8192,256]{1,0:T(8,128)} async-done(((f32[256,256]{1,0:T(8,128)}), f32[8192,256]{1,0:T(8,128)}) %all-gather.9.cloned.1.call-update) | async-done | bytes 8388624 | tf_op jit(solution)/shard_map/while/body/eval_jaxpr/all_gather | solution.py:47
  643.8 3.9 reduce_sum.19
  647.7 0.2 fusion.28
  647.9 0.0 all-gather.9.cloned.1.call-start
  648.0 1.3 dynamic_slice.47
  650.1 0.9 fusion.27
  651.0 0.0 all-gather.9.cloned.1.call-update
  651.0 76.8 %all-gather.9.cloned.1.call-done = f32[8192,256]{1,0:T(8,128)} async-done(((f32[256,256]{1,0:T(8,128)}), f32[8192,256]{1,0:T(8,128)}) %all-gather.9.cloned.1.call-update) | async-done | bytes 8388624 | tf_op jit(solution)/shard_map/while/body/eval_jaxpr/all_gather | solution.py:47
  727.8 3.9 reduce_sum.19
  731.8 0.2 fusion.28
  732.0 0.6 copy-done.1
  (6 shorter events, 0.0 us)
Async XLA Ops:
  6.5 45.5 %all-gather.7.cloned.1.call-start = ((), (), s32[]{:S(2)}) async-start(), calls=%async_computation | async-start | bytes 6553600 | tf_op jit(solution)/shard_map/all_gather | solution.py:24
  7.3 51.9 %copy-start = (f32[1,256,256]{2,1,0:T(8,128)S(1)}, f32[1,256,256]{2,1,0:T(8,128)}, u32[]{:S(2)}) copy-start(f32[1,256,256]{2,1,0:T(8,128)} %param.8) | copy-start | bytes 786436
  7.3 51.9 %copy-start.2 = (bf16[2,1,256,1,256]{4,2,3,1,0:T(8,128)(2,1)S(1)}, bf16[2,1,256,1,256]{4,2,3,1,0:T(8,128)(2,1)}, u32[]{:S(2)}) copy-start(bf16[2,1,256,1,256]{4,2,3,1,0:T(8,128)(2,1)} %param.11) | copy-start | bytes 786436
  7.3 51.9 %copy-start.3 = (bf16[1,256,256]{2,1,0:T(8,128)(2,1)S(1)}, bf16[1,256,256]{2,1,0:T(8,128)(2,1)}, u32[]{:S(2)}) copy-start(bf16[1,256,256]{2,1,0:T(8,128)(2,1)} %param.13) | copy-start | bytes 393220
  59.3 81.3 %all-gather.9.cloned.1.call-start = ((), (), s32[]{:S(2)}) async-start(), calls=%async_computation.1 | async-start | bytes 8650752 | tf_op jit(solution)/shard_map/while/body/eval_jaxpr/all_gather | solution.py:47
  144.7 79.9 %all-gather.9.cloned.1.call-start = ((), (), s32[]{:S(2)}) async-start(), calls=%async_computation.1 | async-start | bytes 8650752 | tf_op jit(solution)/shard_map/while/body/eval_jaxpr/all_gather | solution.py:47
  228.7 79.6 %all-gather.9.cloned.1.call-start = ((), (), s32[]{:S(2)}) async-start(), calls=%async_computation.1 | async-start | bytes 8650752 | tf_op jit(solution)/shard_map/while/body/eval_jaxpr/all_gather | solution.py:47
  312.4 79.6 %all-gather.9.cloned.1.call-start = ((), (), s32[]{:S(2)}) async-start(), calls=%async_computation.1 | async-start | bytes 8650752 | tf_op jit(solution)/shard_map/while/body/eval_jaxpr/all_gather | solution.py:47
  396.2 79.6 %all-gather.9.cloned.1.call-start = ((), (), s32[]{:S(2)}) async-start(), calls=%async_computation.1 | async-start | bytes 8650752 | tf_op jit(solution)/shard_map/while/body/eval_jaxpr/all_gather | solution.py:47
  479.9 79.9 %all-gather.9.cloned.1.call-start = ((), (), s32[]{:S(2)}) async-start(), calls=%async_computation.1 | async-start | bytes 8650752 | tf_op jit(solution)/shard_map/while/body/eval_jaxpr/all_gather | solution.py:47
  563.9 79.9 %all-gather.9.cloned.1.call-start = ((), (), s32[]{:S(2)}) async-start(), calls=%async_computation.1 | async-start | bytes 8650752 | tf_op jit(solution)/shard_map/while/body/eval_jaxpr/all_gather | solution.py:47
  647.9 79.9 %all-gather.9.cloned.1.call-start = ((), (), s32[]{:S(2)}) async-start(), calls=%async_computation.1 | async-start | bytes 8650752 | tf_op jit(solution)/shard_map/while/body/eval_jaxpr/all_gather | solution.py:47
  732.0 0.7 copy-start.1
Sparse Core Ops, SparseCore 0:
  8.9 43.1 all-gather.6
  63.0 77.5 all-gather.8
  148.4 76.1 all-gather.8
  232.1 76.1 all-gather.8
  315.8 76.1 all-gather.8
  399.6 76.1 all-gather.8
  483.6 76.1 all-gather.8
  567.6 76.1 all-gather.8
  651.7 76.1 all-gather.8
